TPU v7x, 512 devices: a whole 4x4x16 slice. The times are simulated.
512 devices in a mesh: dp: 16 (over y, z_hi), tm: 32 (over z_lo, x, core).
Axes of the slice: x: 4, y: 4, z: 16 (z_hi: 4, z_lo: 4; z = z_hi * 4 + z_lo), core: 2. Of those that a mesh axis runs over, the one named last changes fastest.
Arguments:
- frames: bfloat16 [16, 24576, 1536], P('dp', 'tm')
- w_qkv: bfloat16 [1536, 2304], P('dp'), may hold values from -0.15625 to 0.15625
- utt_start: int32 [16, 24], P('dp'), may hold values from 0 to 24447, as said below
- stretch_utt: int32 [16, 96], P('dp'), may hold values from 0 to 23, as said below
- left_stretches: int32 [16, 96], P('dp'), may hold values from 0 to 2, as said below
Outputs:
- context: bfloat16 [16, 24576, 768], P('dp', 'tm')
Inputs may be any that keep to these rules, and one draw needn't show every extreme that they name: `stretch_utt`: in each pack nondecreasing along blocks; utterance u covers one or more whole consecutive blocks; every utterance of 0 to 23 occurs, block 0 in utterance 0. `utt_start`: for utterance u with first block b, at least 256 * b and less than 256 * b + 128. `left_stretches`: at most the number of earlier blocks of the same utterance.
All inputs are finite; a program needn't handle non-finite values.
Results may differ from a plain program's by a relative error of at most 0.0045.
The roundings to bfloat16 on the way count: a program that leaves them out, or rounds other values in their place, can miss the bound.
Values may be sent and summed in bfloat16 or wider, within the bound.
A program may use at most 64 MiB of HBM per device.

v0:
```python
import jax
import jax.numpy as jnp
from jax import lax
from jax.sharding import PartitionSpec as P

HEAD_DIM = 96
STRETCH = 256
LEFT = 2


def from_behind(block, axis, distance):
    devices = range(lax.axis_size(axis))
    route = [(i - distance, i) for i in devices if i - distance in devices]
    return lax.ppermute(block, axis, route)


def attend_block(block_q, window_k, window_v, allowed, live_rows):
    heads = block_q.shape[1] // HEAD_DIM
    qh = block_q.reshape(block_q.shape[0], heads, HEAD_DIM)
    kh = window_k.reshape(window_k.shape[0], heads, HEAD_DIM)
    vh = window_v.reshape(window_v.shape[0], heads, HEAD_DIM)
    scores = jnp.einsum("qhd,khd->hqk", qh, kh, preferred_element_type=jnp.float32) * HEAD_DIM ** (
        -0.5
    )
    scores = jnp.where(allowed[None, :, :], scores, -jnp.inf)
    top = jnp.max(scores, axis=-1, keepdims=True)
    expo = jnp.exp(scores - top)
    probs = (expo / jnp.sum(expo, axis=-1, keepdims=True)).astype(jnp.bfloat16)
    mixed = jnp.einsum("hqk,khd->qhd", probs, vh, preferred_element_type=jnp.float32)
    mixed = mixed.reshape(block_q.shape[0], block_q.shape[1])
    return jnp.where(live_rows[:, None], mixed, jnp.zeros_like(mixed)).astype(jnp.bfloat16)


def local(frames, w_qkv, utt_start, stretch_utt, left_stretches):
    inputs = frames[0]
    rows = inputs.shape[0]
    width = w_qkv.shape[1]
    inner = width // 3
    projected = jnp.dot(
        inputs, lax.all_gather(w_qkv, "dp", axis=0, tiled=True), preferred_element_type=jnp.float32
    )
    qkv = projected.astype(jnp.bfloat16)
    query = qkv[:, :inner]
    keys = qkv[:, inner : 2 * inner]
    values = qkv[:, 2 * inner :]
    reach = LEFT * STRETCH
    halo_keys, halo_values = from_behind((keys[rows - reach :], values[rows - reach :]), "tm", 1)
    blocks = rows // STRETCH
    first = lax.axis_index("tm") * blocks
    extended = first - LEFT + jnp.arange(blocks + LEFT, dtype=jnp.int32)
    table = jnp.arange(stretch_utt.shape[1], dtype=jnp.int32)
    onehot = extended[:, None] == table[None, :]
    ext_owner = jnp.where(
        extended >= 0, jnp.sum(jnp.where(onehot, stretch_utt[0][None, :], 0), axis=1), -1
    )
    ext_left = jnp.sum(jnp.where(onehot, left_stretches[0][None, :], 0), axis=1)
    utt_ids = jnp.arange(utt_start.shape[1], dtype=jnp.int32)
    ext_start = jnp.sum(
        jnp.where(ext_owner[:, None] == utt_ids[None, :], utt_start[0][None, :], 0), axis=1
    )
    frame_pos = (first - LEFT) * STRETCH + jnp.arange((blocks + LEFT) * STRETCH, dtype=jnp.int32)
    key_live = (frame_pos >= jnp.repeat(ext_start, STRETCH)) & jnp.repeat(extended >= 0, STRETCH)
    query_live = key_live[reach:]
    own = jnp.arange(blocks, dtype=jnp.int32) + LEFT
    column = jnp.arange(blocks + LEFT, dtype=jnp.int32)
    block_ok = ext_owner[LEFT:][:, None] == ext_owner[None, :]
    block_ok = (
        block_ok
        & (column[None, :] >= (own - ext_left[LEFT:])[:, None])
        & (column[None, :] <= own[:, None])
    )
    usable = jnp.repeat(jnp.repeat(block_ok, STRETCH, axis=0), STRETCH, axis=1) & key_live[None, :]
    span = reach + STRETCH

    def block_inputs(block):
        block_q = lax.dynamic_slice_in_dim(query, block * STRETCH, STRETCH, 0)
        allowed = lax.dynamic_slice(usable, (block * STRETCH, block * STRETCH), (STRETCH, span))
        live_rows = lax.dynamic_slice_in_dim(query_live, block * STRETCH, STRETCH, 0)
        return (block_q, allowed, live_rows)

    output = jnp.zeros((rows, inner), jnp.bfloat16)
    all_keys = jnp.concatenate([halo_keys, keys], axis=0)
    all_values = jnp.concatenate([halo_values, values], axis=0)

    def joined_step(block, result):
        block_q, allowed, live_rows = block_inputs(block)
        window_k = lax.dynamic_slice_in_dim(all_keys, block * STRETCH, span, 0)
        window_v = lax.dynamic_slice_in_dim(all_values, block * STRETCH, span, 0)
        mixed = attend_block(block_q, window_k, window_v, allowed, live_rows)
        return lax.dynamic_update_slice_in_dim(result, mixed, block * STRETCH, 0)

    output = lax.fori_loop(0, blocks, joined_step, output)
    return output[None]


def solution(mesh):
    return jax.shard_map(
        local,
        mesh=mesh,
        in_specs=(P("dp", "tm", None), P("dp", None), P("dp", None), P("dp", None), P("dp", None)),
        out_specs=P("dp", "tm", None),
        check_vma=False,
    )
```

profile of v0, /device:TPU:1, one launch (start us, length us, event | category | flops | bytes accessed | tf_op | source)
XLA Modules:
  0.0 320.1 jit_solution(3534528538389036803)
XLA Ops:
  6.5 0.0 copy-start
  6.5 0.7 all-gather.2.cloned.1.call-update
  7.3 0.1 broadcast_in_dim.130
  7.4 0.9 select_reduce_fusion
  8.3 0.1 slice.29
  8.3 0.8 select_reduce_fusion.1
  9.2 0.1 broadcast_in_dim.129
  9.3 0.1 slice_subtract_fusion
  9.4 195.2 %all-gather.2.cloned.1.call-done = bf16[1536,2304]{1,0:T(8,128)(2,1)} async-done(((bf16[96,2304]{1,0:T(8,128)(2,1)}), bf16[1536,2304]{1,0:T(8,128)(2,1)}) %all-gather.2.cloned.1.call-update) | async-done | bytes 7077904 | tf_op jit(solution)/shard_map/all_gather | solution.py:40
  204.5 8.8 %convolution_convert_fusion = bf16[768,2304]{1,0:T(8,128)(2,1)S(1)} fusion(bf16[1536,2304]{1,0:T(8,128)(2,1)} %all-gather.2.cloned.1.call-done, bf16[1,768,1536]{2,1,0:T(8,128)(2,1)S(1)} %copy-done), kind=kOutput, calls=%fused_computation.18 | convolution fusion | flops 5437587456 | bytes 12976128 | tf_op jit(solution)/shard_map/dot_general | solution.py:39
  213.4 0.1 fusion.16
  213.5 3.5 %collective-permute-start = (bf16[512,768]{1,0:T(8,128)(2,1)S(1)}, bf16[512,768]{1,0:T(8,128)(2,1)S(1)}, u32[]{:S(2)}, u32[]{:S(2)}) collective-permute-start(bf16[512,768]{1,0:T(8,128)(2,1)S(1)} %get-tuple-element.172), channel_id=1, source_target_pairs={{0,1},{1,2},{2,3},{3,4},{4,5},{5,6},{6,7},{7,8},{8,9},{9,10},{10,1... | collective-permute-start | bytes 2359304 | tf_op jit(solution)/shard_map/ppermute | solution.py:14
  217.0 0.1 fusion.14
  217.0 2.0 collective-permute-start.1
  219.0 0.1 broadcast_bitcast_fusion
  219.1 1.5 bitcast_and_fusion
  220.5 1.2 fusion.17
  221.8 4.1 %collective-permute-done = bf16[512,768]{1,0:T(8,128)(2,1)S(1)} collective-permute-done((bf16[512,768]{1,0:T(8,128)(2,1)S(1)}, bf16[512,768]{1,0:T(8,128)(2,1)S(1)}, u32[]{:S(2)}, u32[]{:S(2)}) %collective-permute-start) | collective-permute-done | bytes 786464 | tf_op jit(solution)/shard_map/ppermute | solution.py:14
  225.9 1.4 pad_maximum_fusion
  227.3 7.0 %collective-permute-done.1 = bf16[512,768]{1,0:T(8,128)(2,1)S(1)} collective-permute-done((bf16[512,768]{1,0:T(8,128)(2,1)S(1)}, bf16[512,768]{1,0:T(8,128)(2,1)S(1)}, u32[]{:S(2)}, u32[]{:S(2)}) %collective-permute-start.1) | collective-permute-done | bytes 786464 | tf_op jit(solution)/shard_map/ppermute | solution.py:14
  234.3 1.5 pad_maximum_fusion.1
  235.8 1.1 broadcast_in_dim.121.clone
  236.9 76.4 %while.13 = (s32[]{:T(128)}, bf16[768,768]{1,0:T(8,128)(2,1)}, pred[768]{0:T(1024)(128)(4,1)S(1)}, bf16[1280,768]{1,0:T(8,128)(2,1)}, pred[768,1280]{0,1:T(8,128...) while((s32[]{:T(128)}, bf16[768,768]{1,0:T(8,128)(2,1)}, ...), condition=%wide.region_6.7_spmd, body=%wide.region_3.6_spmd.sunk | while | flops 613614336 | bytes 34817012 | solution.py:92
  236.9 2.8 constant_dynamic-slice_fusion.5
  239.6 2.4 copy.32
  242.0 1.6 dynamic_slice.44
  243.7 1.9 copy.33
  245.5 1.8 constant_dynamic-slice_fusion.6
  247.3 1.9 copy.34
  249.2 1.5 copy.35
  250.7 6.5 %fusion.33 = (f32[8,256]{1,0:T(8,128)S(1)}, f32[8,256,768]{2,1,0:T(8,128)}) fusion(pred[256,768]{1,0:T(8,128)(4,1)} %copy.33, bf16[256,8,96]{0,2,1:T(8,128)(2,1)} %bitcast.45, bf16[768,8,96]{0,2,1:T(8,128)(2,1)} %bitcast.44), kind=kOutput, calls=%fused_computation.40.clone.1 | convolution fusion | flops 308282112 | bytes 8069120 | tf_op jit(solution)/shard_map/while/body/eval_jaxpr/sub | solution.py:27
  257.2 4.0 %fusion.34 = bf16[8,96,256]{2,1,0:T(8,128)(2,1)S(1)} fusion(bf16[768,8,96]{0,2,1:T(8,128)(2,1)S(1)} %bitcast.43, f32[8,256,768]{2,1,0:T(8,128)} %get-tuple-element.227, f32[8,256]{1,0:T(8,128)S(1)} %get-tuple-element.228), kind=kOutput, calls=%fused_computation.7.clone.1 | convolution fusion | flops 305135616 | bytes 7872512 | tf_op jit(solution)/shard_map/while/body/eval_jaxpr/hqk,khd->qhd/dot_general | solution.py:29
  261.2 0.1 dynamic_slice.45
  261.3 0.1 fusion.35
  261.4 0.2 copy.36
  261.6 0.8 constant_dynamic-update-slice_fusion.2
  262.3 2.8 constant_dynamic-slice_fusion.5
  265.1 2.4 copy.32
  267.5 1.6 dynamic_slice.44
  269.1 1.9 copy.33
  271.0 1.8 constant_dynamic-slice_fusion.6
  272.8 1.9 copy.34
  274.7 1.5 copy.35
  276.2 6.5 %fusion.33 = (f32[8,256]{1,0:T(8,128)S(1)}, f32[8,256,768]{2,1,0:T(8,128)}) fusion(pred[256,768]{1,0:T(8,128)(4,1)} %copy.33, bf16[256,8,96]{0,2,1:T(8,128)(2,1)} %bitcast.45, bf16[768,8,96]{0,2,1:T(8,128)(2,1)} %bitcast.44), kind=kOutput, calls=%fused_computation.40.clone.1 | convolution fusion | flops 308282112 | bytes 8069120 | tf_op jit(solution)/shard_map/while/body/eval_jaxpr/sub | solution.py:27
  282.7 0.0 copy-done.1
  282.7 4.0 %fusion.34 = bf16[8,96,256]{2,1,0:T(8,128)(2,1)S(1)} fusion(bf16[768,8,96]{0,2,1:T(8,128)(2,1)S(1)} %bitcast.43, f32[8,256,768]{2,1,0:T(8,128)} %get-tuple-element.227, f32[8,256]{1,0:T(8,128)S(1)} %get-tuple-element.228), kind=kOutput, calls=%fused_computation.7.clone.1 | convolution fusion | flops 305135616 | bytes 7872512 | tf_op jit(solution)/shard_map/while/body/eval_jaxpr/hqk,khd->qhd/dot_general | solution.py:29
  286.7 0.1 dynamic_slice.45
  286.8 0.1 fusion.35
  286.9 0.2 copy.36
  287.0 0.8 constant_dynamic-update-slice_fusion.2
  287.8 2.8 constant_dynamic-slice_fusion.5
  290.6 2.4 copy.32
  293.0 1.6 dynamic_slice.44
  294.6 1.9 copy.33
  296.5 1.8 constant_dynamic-slice_fusion.6
  298.3 1.9 copy.34
  300.2 1.5 copy.35
  301.7 6.5 %fusion.33 = (f32[8,256]{1,0:T(8,128)S(1)}, f32[8,256,768]{2,1,0:T(8,128)}) fusion(pred[256,768]{1,0:T(8,128)(4,1)} %copy.33, bf16[256,8,96]{0,2,1:T(8,128)(2,1)} %bitcast.45, bf16[768,8,96]{0,2,1:T(8,128)(2,1)} %bitcast.44), kind=kOutput, calls=%fused_computation.40.clone.1 | convolution fusion | flops 308282112 | bytes 8069120 | tf_op jit(solution)/shard_map/while/body/eval_jaxpr/sub | solution.py:27
  308.2 0.0 copy-done.1
  308.2 4.0 %fusion.34 = bf16[8,96,256]{2,1,0:T(8,128)(2,1)S(1)} fusion(bf16[768,8,96]{0,2,1:T(8,128)(2,1)S(1)} %bitcast.43, f32[8,256,768]{2,1,0:T(8,128)} %get-tuple-element.227, f32[8,256]{1,0:T(8,128)S(1)} %get-tuple-element.228), kind=kOutput, calls=%fused_computation.7.clone.1 | convolution fusion | flops 305135616 | bytes 7872512 | tf_op jit(solution)/shard_map/while/body/eval_jaxpr/hqk,khd->qhd/dot_general | solution.py:29
  312.1 0.1 dynamic_slice.45
  312.2 0.1 fusion.35
  312.3 0.2 copy.36
  312.5 0.8 constant_dynamic-update-slice_fusion.2
  (14 shorter events, 0.1 us)
Async XLA Ops:
  6.5 198.0 %copy-start = (bf16[1,768,1536]{2,1,0:T(8,128)(2,1)S(1)}, bf16[1,768,1536]{2,1,0:T(8,128)(2,1)}, u32[]{:S(2)}) copy-start(bf16[1,768,1536]{2,1,0:T(8,128)(2,1)} %param.7) | copy-start | bytes 7077892
  6.5 198.0 %all-gather.2.cloned.1.call-start = ((), (), s32[]{:S(2)}) async-start(), calls=%async_computation | async-start | bytes 7520256 | tf_op jit(solution)/shard_map/all_gather | solution.py:40
  213.5 12.4 %collective-permute-start = (bf16[512,768]{1,0:T(8,128)(2,1)S(1)}, bf16[512,768]{1,0:T(8,128)(2,1)S(1)}, u32[]{:S(2)}, u32[]{:S(2)}) collective-permute-start(bf16[512,768]{1,0:T(8,128)(2,1)S(1)} %get-tuple-element.172), channel_id=1, source_target_pairs={{0,1},{1,2},{2,3},{3,4},{4,5},{5,6},{6,7},{7,8},{8,9},{9,10},{10,1... | collective-permute-start | bytes 2359304 | tf_op jit(solution)/shard_map/ppermute | solution.py:14
  217.0 17.3 %collective-permute-start.1 = (bf16[512,768]{1,0:T(8,128)(2,1)S(1)}, bf16[512,768]{1,0:T(8,128)(2,1)S(1)}, u32[]{:S(2)}, u32[]{:S(2)}) collective-permute-start(bf16[512,768]{1,0:T(8,128)(2,1)S(1)} %get-tuple-element.171), channel_id=1, source_target_pairs={{0,1},{1,2},{2,3},{3,4},{4,5},{5,6},{6,7},{7,8},{8,9},{9,10},{10,1... | collective-permute-start | bytes 2359304 | tf_op jit(solution)/shard_map/ppermute | solution.py:14
  250.7 6.5 %copy-start.1 = (bf16[768,768]{0,1:T(8,128)(2,1)S(1)}, bf16[768,768]{0,1:T(8,128)(2,1)}, u32[]{:S(2)}) copy-start(bf16[768,768]{0,1:T(8,128)(2,1)} %copy.32) | copy-start | bytes 3538948 | tf_op jit(solution)/shard_map/while
  276.2 6.5 %copy-start.1 = (bf16[768,768]{0,1:T(8,128)(2,1)S(1)}, bf16[768,768]{0,1:T(8,128)(2,1)}, u32[]{:S(2)}) copy-start(bf16[768,768]{0,1:T(8,128)(2,1)} %copy.32) | copy-start | bytes 3538948 | tf_op jit(solution)/shard_map/while
  301.7 6.5 %copy-start.1 = (bf16[768,768]{0,1:T(8,128)(2,1)S(1)}, bf16[768,768]{0,1:T(8,128)(2,1)}, u32[]{:S(2)}) copy-start(bf16[768,768]{0,1:T(8,128)(2,1)} %copy.32) | copy-start | bytes 3538948 | tf_op jit(solution)/shard_map/while
Sparse Core Ops, SparseCore 0:
  10.4 194.0 all-gather.1
where the time goes:
time: 321 us; the launch traced here: 320 us
  waiting for transfers between devices  207 us (64%)
  local copies, waits for them, and re-layouts  47.4 us (15%)
  matrix products  40.2 us (13%)
  between operations  13.5 us (4%)
  other arithmetic  6.55 us (2%)
  starting transfers between devices  5.43 us (2%)
    all_gather x1, waiting for transfers between devices, local(): lax.all_gather(w_qkv, 'dp', axis=0, tiled=True)  195 us
    sub x3, matrix products, attend_block(): expo = jnp.exp(scores - top)  19.5 us
    dynamic_slice x6, local copies, waits for them, and re-layouts, joined_step(): window_k = lax.dynamic_slice_in_dim(all_keys, block * STRETCH, span, 0)  12.8 us
    dot_general x3, matrix products, attend_block(): jnp.einsum('hqk,khd->qhd', probs, vh, preferred_element_type=jnp.float32)  11.9 us
    dynamic_slice x6, local copies, waits for them, and re-layouts, block_inputs(): block_q = lax.dynamic_slice_in_dim(query, block * STRETCH, STRETCH, 0)  11.2 us
    ppermute x2, waiting for transfers between devices, from_behind(): return lax.ppermute(block, axis, route)  11.1 us
    dynamic_slice x6, local copies, waits for them, and re-layouts, block_inputs(): lax.dynamic_slice(usable, (block * STRETCH, block * STRETCH), (STRETCH, s...  10.5 us
    dot_general x1, matrix products, local(): jnp.dot(inputs, lax.all_gather(w_qkv, 'dp', axis=0, tiled=True), preferre...  8.83 us
  transfers between devices with their start and end apart: 3, of which 3 were waited for; matrix products, arithmetic and copies ran while one was open for 2% of the time, Pallas kernels for 0%

commit v1 on v0

v1 whole, which is shorter than its diff:
```python
import functools

import jax
import jax.numpy as jnp
from jax import lax
from jax.experimental import pallas as pl
from jax.experimental.pallas import tpu as pltpu
from jax.sharding import PartitionSpec as P

MESH = pl.DeviceIdType.MESH
BF16, F32 = jnp.bfloat16, jnp.float32
HEAD_DIM = 96
STRETCH = 256
ROWS = 768
CHIP = 1536
REACH = 512
DEPTH = 96
HALF = 48
COLS = 384
CHUNKS = 3
LAG = 3
SCALE = HEAD_DIM**-0.5 * 1.4426950408889634


def place():
    dp, tm = lax.axis_index("dp"), lax.axis_index("tm")
    return dp // 4, dp % 4, tm // 8, (tm // 2) % 4, tm % 2


def device(y, z, x, core):
    y, z, x = (y + 4) % 4, (z + 16) % 16, (x + 4) % 4
    return (y * 4 + z // 4, (z % 4) * 8 + x * 2 + core)


def remote(src, dst, send, recv, target):
    return pltpu.make_async_remote_copy(
        src_ref=src, dst_ref=dst, send_sem=send, recv_sem=recv, device_id=target, device_id_type=MESH
    )


def unit_at(p):
    q = p - 15
    relay = p >= 15
    chunk = jnp.where(relay, jnp.where(q < 6, q // 3, 2), p // 5)
    kind = jnp.where(relay, 5 + q % 3, p % 5)
    ok = (p >= 0) & (p < 27) & ((q < 6) | (q >= 9))
    return chunk, kind, ok


def kernel(
    x_hbm, w_hbm, start_ref, utt_ref, left_ref, out_hbm,
    xb, wb, qb, kb, vb, ob,
    lx, lw, cs, cr, hs, hr, gs, gr, zs, zr, ys, yr, bs, br, os_, or_, lo,
):
    y, zh, zl, x, core = place()
    z = zh * 4 + zl
    me = device(y, z, x, core)
    sibling = (me[0], me[1] + 1 - 2 * core)
    y_near = [device(y + d, z, x, core) for d in (1, 3, 2)]
    up, down = device(y, z + 1, x, core), device(y, z - 1, x, core)
    tm = me[1]
    chip = tm // 2
    nxt = (chip + 1) % 16
    prv = (chip + 15) % 16

    def rows_of(yy, zz, half):
        return pl.multiple_of(((yy % 4) * 4 + (zz % 4)) * DEPTH + half * HALF, 16)

    barrier = pltpu.get_barrier_semaphore()

    def greet(target):
        pl.semaphore_signal(barrier, inc=1, device_id=target, device_id_type=MESH)

    own_rows = pl.ds(rows_of(y, zh, 0), DEPTH)
    for k in range(CHUNKS):
        for j in range(3):
            col = pl.multiple_of(j * 768 + core * 384 + k * 128, 128)
            pltpu.make_async_copy(
                w_hbm.at[:, pl.ds(col, 128)], wb.at[k, own_rows, pl.ds(j * 128, 128)], lw.at[k, j]
            ).start()
    own_x = pl.ds(pl.multiple_of(REACH + core * ROWS, 16), ROWS)
    own_frames = pltpu.make_async_copy(x_hbm.at[0], xb.at[own_x], lx.at[0])
    own_frames.start()

    for t in y_near + [up, down, sibling]:
        greet(t)
    greet((me[0], prv * 2 + 1))

    @pl.when(core == 1)
    def _():
        greet((me[0], nxt * 2))
        greet((me[0], nxt * 2 + 1))

    pl.semaphore_wait(barrier, 7 + 2 * core)

    for k in range(CHUNKS):
        for j in range(3):
            pltpu.make_async_copy(
                w_hbm.at[:, pl.ds(0, 128)], wb.at[k, own_rows, pl.ds(j * 128, 128)], lw.at[k, j]
            ).wait()

    def y_own(k, i):
        part = wb.at[k, own_rows]
        return remote(part, part, ys.at[k, i], yr.at[k, i], y_near[i])

    for k in range(CHUNKS):
        for i in range(3):
            y_own(k, i).start()

    to_sibling = remote(x_hbm.at[0], xb.at[own_x], cs.at[0], cr.at[0], sibling)
    to_sibling.start()
    has_next = (core == 1) & (chip < 15)
    has_prev = chip > 0

    def halo(i):
        return remote(
            x_hbm.at[0, pl.ds(STRETCH * (i + 1), STRETCH)], xb.at[pl.ds(STRETCH * i, STRETCH)],
            hs.at[i], hr.at[0], (me[0], nxt * 2 + i),
        )

    @pl.when(has_next)
    def _():
        halo(0).start()
        halo(1).start()

    def y_own_wait(k, i):
        rows = pl.ds(rows_of(y - (1, 3, 2)[i] + 4, zh, 0), DEPTH)
        part = wb.at[k, rows]
        remote(part, part, ys.at[k, i], yr.at[k, i], y_near[i]).wait_recv()

    def unit(sign, k, kind, receiver):
        far = kind >= 5
        group = receiver - sign * jnp.where(far, 2, 1) + 8
        if sign > 0:
            off = jnp.where((kind == 2) | (kind == 7), 1, jnp.where(kind == 3, 3, jnp.where(kind == 4, 2, 0)))
        else:
            off = jnp.where(
                (kind == 2) | (kind == 6), 3, jnp.where((kind == 3) | (kind == 7), 2, jnp.where(kind == 4, 1, 0))
            )
        half = jnp.where((kind == 0) | (kind == 5), 1, 0)
        return wb.at[k, pl.ds(rows_of(y + off, group, half), HALF)], group

    def z_copy(sign, k, kind, receiver):
        part, _ = unit(sign, k, kind, receiver)
        d = (1 - sign) // 2
        n = k * 8 + kind
        return remote(part, part, zs.at[d, n], zr.at[d, n], up if sign > 0 else down)

    def used(sign, k, kind):
        even = (y + k) % 2 == 0
        return (kind != 5) | (even if sign > 0 else jnp.logical_not(even))

    def y_part(k, kind_group, i):
        part = wb.at[k, pl.ds(rows_of(y, kind_group, 1), HALF)]
        slot = (kind_group - zh + 8) % 4 - 1
        return remote(part, part, bs.at[k, slot, i], br.at[k, slot, i], y_near[i])

    def step(s):
        for sign in (1, -1):
            edge = zl == (3 if sign > 0 else 0)
            hop = zl + 1 if sign > 0 else 4 - zl
            k0, kind0, ok0 = unit_at(s)

            @pl.when(edge & ok0 & (kind0 < 5))
            def _():
                z_copy(sign, k0, kind0, zh + sign + 4).start()

            k, kind, ok = unit_at(s - hop * LAG)

            @pl.when(ok & used(sign, k, kind))
            def _():
                z_copy(sign, k, kind, zh + 4).wait_recv()

                @pl.when(jnp.logical_not(edge))
                def _():
                    z_copy(sign, k, kind, zh + 4).start()

                if sign > 0:
                    relays, relay = kind <= 2, kind + 5
                else:
                    relays = (kind == 0) | (kind == 2) | (kind == 3)
                    relay = jnp.where(kind == 0, 5, kind + 4)

                @pl.when(edge & relays & used(sign, k, relay))
                def _():
                    z_copy(sign, k, relay, zh + sign + 4).start()

                @pl.when((kind == 0) | (kind == 5))
                def _():
                    group = (zh - sign * jnp.where(kind == 5, 2, 1) + 8) % 4
                    for i in range(3):
                        y_part(k, group, i).start()

    for k in range(CHUNKS):
        for i in range(3):
            y_own_wait(k, i)

    @pl.loop(0, 27 + 4 * LAG)
    def _(s):
        step(s)

    @pl.when(has_prev)
    def _():
        part = xb.at[pl.ds(pl.multiple_of(STRETCH * core, 16), STRETCH)]
        remote(part, part, gs.at[0], hr.at[0], sibling).wait_recv()
        remote(part, part, gs.at[0], gr.at[0], sibling).start()

    @pl.when(jnp.logical_not(has_prev))
    def _():
        xb[0:REACH] = jnp.zeros((REACH, xb.shape[1]), BF16)

    own_frames.wait()
    other_x = xb.at[pl.ds(pl.multiple_of(REACH + (1 - core) * ROWS, 16), ROWS)]
    remote(other_x, other_x, cs.at[0], cr.at[0], sibling).wait_recv()

    for k in range(CHUNKS):
        for slot in range(3):
            for i in range(3):
                part = wb.at[k, pl.ds(rows_of(y - (1, 3, 2)[i] + 4, zh + slot + 1, 1), HALF)]
                remote(part, part, bs.at[k, slot, i], br.at[k, slot, i], y_near[i]).wait_recv()

    @pl.when(has_prev)
    def _():
        part = xb.at[pl.ds(pl.multiple_of(STRETCH * (1 - core), 16), STRETCH)]
        remote(part, part, gs.at[0], gr.at[0], sibling).wait_recv()

    @pl.loop(0, 8)
    def _(r):
        rr = pl.ds(pl.multiple_of(r * STRETCH, STRETCH), STRETCH)
        a = xb[rr, :]
        for k in range(CHUNKS):
            p = jnp.dot(a, wb[k], preferred_element_type=F32).astype(BF16)
            to = slice(k * 128, (k + 1) * 128)
            qb[rr, to] = p[:, 0:128]
            kb[rr, to] = p[:, 128:256]
            vb[rr, to] = p[:, 256:384]

    lane = lax.broadcasted_iota(jnp.int32, (1, 128), 1)

    def attend(h, b, bias):
        t0, t1 = (h * HEAD_DIM) // 128, (h * HEAD_DIM + HEAD_DIM - 1) // 128
        width = (t1 - t0 + 1) * 128
        low = h * HEAD_DIM - t0 * 128
        lanes = lax.broadcasted_iota(jnp.int32, (1, width), 1)
        mine = (lanes >= low) & (lanes < low + HEAD_DIM)
        rq = pl.ds(pl.multiple_of((b + 2) * STRETCH, STRETCH), STRETCH)
        rk = pl.ds(pl.multiple_of(b * STRETCH, STRETCH), 3 * STRETCH)
        cols = slice(t0 * 128, t0 * 128 + width)
        q = jnp.where(mine, qb[rq, cols], jnp.zeros((), BF16))
        v = jnp.where(mine, vb[rk, cols], jnp.ones((), BF16))
        s = lax.dot_general(q, kb[rk, cols], (((1,), (1,)), ((), ())), preferred_element_type=F32)
        s = s + bias
        m = jnp.max(s, axis=1, keepdims=True)
        e = jnp.exp2((s - m) * SCALE).astype(BF16)
        o = jnp.dot(e, v, preferred_element_type=F32)
        one = 0 if low > 0 else HEAD_DIM
        return o / o[:, one : one + 1]

    def out_local(b, to):
        rr = pl.ds(pl.multiple_of(b * STRETCH, STRETCH), STRETCH)
        ro = pl.ds(pl.multiple_of(to * STRETCH, STRETCH), STRETCH)
        mine = out_hbm.at[0, ro, pl.ds(pl.multiple_of(core * COLS, 128), COLS)]
        return rr, mine

    @pl.loop(0, 6)
    def _(b):
        block = chip * 6 + b
        owner = utt_ref[0, block]
        reach = left_ref[0, block]
        start = start_ref[0, owner]
        parts = []
        for d in (2, 1, 0):
            j = block - d
            ok = (j >= 0) & (utt_ref[0, jnp.maximum(j, 0)] == owner) & (reach >= d)
            pos = j * STRETCH + lax.broadcasted_iota(jnp.int32, (1, STRETCH), 1)
            first = jnp.where(ok, start, 1 << 30)
            parts.append(jnp.where(pos >= first, 0.0, -jnp.inf).astype(F32))
        bias = jnp.concatenate(parts, axis=1)
        live = block * STRETCH + lax.broadcasted_iota(jnp.int32, (STRETCH, 1), 0) >= start
        o0, o1, o2, o3 = [attend(h, b, bias) for h in range(4)]
        rr = pl.ds(pl.multiple_of(b * STRETCH, STRETCH), STRETCH)
        zero = jnp.zeros((), F32)
        ob[rr, 0:128] = jnp.where(live, jnp.where(lane < 96, o0, o1[:, :128]), zero).astype(BF16)
        ob[rr, 128:256] = jnp.where(live, jnp.where(lane < 64, o1[:, 128:], o2[:, :128]), zero).astype(BF16)
        ob[rr, 256:384] = jnp.where(live, jnp.where(lane < 32, o2[:, 128:], o3), zero).astype(BF16)
        i = b % 3
        src, dst = out_local(b, i)
        here = (b // 3) == core

        @pl.when(here)
        def _():
            pltpu.make_async_copy(ob.at[src], dst, lo.at[i]).start()

        @pl.when(jnp.logical_not(here))
        def _():
            remote(ob.at[src], dst, os_.at[i], or_.at[i], sibling).start()

    for i in range(3):
        src, dst = out_local(i, i)
        pltpu.make_async_copy(ob.at[src], dst, lo.at[i]).wait()
        other = out_hbm.at[0, pl.ds(i * STRETCH, STRETCH), pl.ds(pl.multiple_of((1 - core) * COLS, 128), COLS)]
        c = remote(ob.at[src], other, os_.at[i], or_.at[i], sibling)
        c.wait_send()
        c.wait_recv()
    for k in range(CHUNKS):
        for i in range(3):
            y_own(k, i).wait_send()
        for slot in range(3):
            for i in range(3):
                part = wb.at[k, pl.ds(0, HALF)]
                remote(part, part, bs.at[k, slot, i], br.at[k, slot, i], y_near[i]).wait_send()
        for sign in (1, -1):
            for kind in range(8):

                def drain(sign=sign, k=k, kind=kind):
                    z_copy(sign, k, kind, zh + 4).wait_send()

                if kind == 5:
                    pl.when(used(sign, k, kind))(drain)
                else:
                    drain()
    to_sibling.wait_send()

    @pl.when(has_next)
    def _():
        halo(0).wait_send()
        halo(1).wait_send()

    @pl.when(has_prev)
    def _():
        part = xb.at[pl.ds(pl.multiple_of(STRETCH * core, 16), STRETCH)]
        remote(part, part, gs.at[0], gr.at[0], sibling).wait_send()


def local(frames, w_qkv, utt_start, stretch_utt, left_stretches):
    any_ = pl.BlockSpec(memory_space=pl.ANY)
    smem = pl.BlockSpec(memory_space=pltpu.SMEM)
    dma = pltpu.SemaphoreType.DMA
    return pl.pallas_call(
        kernel,
        out_shape=jax.ShapeDtypeStruct((1, ROWS, 768), BF16),
        in_specs=[any_, any_, smem, smem, smem],
        out_specs=any_,
        scratch_shapes=[
            pltpu.VMEM((REACH + CHIP, 1536), BF16),
            pltpu.VMEM((CHUNKS, 1536, COLS), BF16),
            pltpu.VMEM((REACH + CHIP, COLS), BF16),
            pltpu.VMEM((REACH + CHIP, COLS), BF16),
            pltpu.VMEM((REACH + CHIP, COLS), BF16),
            pltpu.VMEM((CHIP, COLS), BF16),
            dma((1,)), dma((CHUNKS, 3)),
            dma((1,)), dma((1,)), dma((2,)), dma((1,)), dma((1,)), dma((1,)),
            dma((2, 24)), dma((2, 24)), dma((CHUNKS, 3)), dma((CHUNKS, 3)),
            dma((CHUNKS, 3, 3)), dma((CHUNKS, 3, 3)),
            dma((3,)), dma((3,)), dma((3,)),
        ],
        compiler_params=pltpu.CompilerParams(
            collective_id=0, has_side_effects=True, vmem_limit_bytes=60 << 20
        ),
        name="block_attention",
    )(frames, w_qkv, utt_start, stretch_utt, left_stretches)


def solution(mesh):
    return jax.shard_map(
        local,
        mesh=mesh,
        in_specs=(P("dp", "tm", None), P("dp", None), P("dp", None), P("dp", None), P("dp", None)),
        out_specs=P("dp", "tm", None),
        check_vma=False,
    )
```

time: 321 us -> 94 us (0.29)
  waiting for transfers between devices: 207 us -> 0 us
  Pallas kernels: 0 us -> 91.5 us
  local copies, waits for them, and re-layouts: 47.4 us -> 2.36 us
  matrix products: 40.2 us -> 0 us
  between operations: 13.5 us -> 0.01 us
  other arithmetic: 6.55 us -> 0 us
  starting transfers between devices: 5.43 us -> 0 us
    all_gather x1 -> x0, waiting for transfers between devices: 195 us -> none  [local(): lax.all_gather(w_qkv, 'dp', axis=0, tiled=True)]
    pallas_call x0 -> x1, Pallas kernels: none -> 91.5 us  [local(): pl.pallas_call(kernel, out_shape=jax.ShapeDtypeStruct((1, ROWS, 768), BF1...]
    dynamic_slice x24 -> x0, local copies, waits for them, and re-layouts: 41.8 us -> none  [the longest x6 12.8 us: joined_step(): window_k = lax.dynamic_slice_in_dim(all_keys, block * STRETCH, span, 0)]
    dot_general x4 -> x0, matrix products: 20.7 us -> none  [the longest x3 11.9 us: attend_block(): jnp.einsum('hqk,khd->qhd', probs, vh, preferred_element_type=jnp.float32)]
    sub x3 -> x0, matrix products: 19.5 us -> none  [attend_block(): expo = jnp.exp(scores - top)]
    ppermute x2 -> x0, waiting for transfers between devices: 11.1 us -> none  [from_behind(): return lax.ppermute(block, axis, route)]
    ppermute x2 -> x0, starting transfers between devices: 5.42 us -> none  [from_behind(): return lax.ppermute(block, axis, route)]
  transfers between devices with their start and end apart: 3 -> 0, of which waited for: 3 -> 0; matrix products, arithmetic and copies ran while one was open for 2% -> 0% of each run, Pallas kernels for 0% -> 0%
where the time goes in v1:
time: 94 us; the launch traced here: 93.8 us
  Pallas kernels  91.5 us (97%)
  local copies, waits for them, and re-layouts  2.36 us (3%)
    pallas_call x1, Pallas kernels, local(): pl.pallas_call(kernel, out_shape=jax.ShapeDtypeStruct((1, ROWS, 768), BF1...  91.5 us
    unnamed x1, local copies, waits for them, and re-layouts  2.36 us

profile of v1, /device:TPU:1, one launch (start us, length us, event | category | flops | bytes accessed | tf_op | source)
XLA Modules:
  0.0 93.8 jit_solution(2885624624603436169)
XLA Ops:
  0.0 91.5 %block_attention.1 = bf16[1,768,768]{2,1,0:T(8,128)(2,1)} custom-call(bf16[1,768,1536]{2,1,0:T(8,128)(2,1)} %x_hbm.1, bf16[96,2304]{1,0:T(8,128)(2,1)} %w_hbm.1, s32[1,24]{1,0:T(1,128)} %start_ref.1, s32[1,96]{1,0:T(1,128)} %utt_ref.1, s32[1,96]{1,0:T(1,128)} %left_ref.1), custom_call_target="tpu_custom_call" | custom-call | tf_op jit(solution)/shard_map/block_attention/pallas_call | solution.py:339
  91.5 2.4 %copy.7 = bf16[1,768,768]{2,1,0:T(8,128)(2,1)} copy(bf16[1,768,768]{2,1,0:T(8,128)(2,1)} %block_attention.1) | data formatting | bytes 2359296

commit v2 on v0

v2 whole, which is shorter than its diff:
```python
import functools

import jax
import jax.numpy as jnp
from jax import lax
from jax.experimental import pallas as pl
from jax.experimental.pallas import tpu as pltpu
from jax.sharding import PartitionSpec as P

MESH = pl.DeviceIdType.MESH
BF16, F32 = jnp.bfloat16, jnp.float32
HEAD_DIM = 96
STRETCH = 256
ROWS = 768
CHIP = 1536
REACH = 512
DEPTH = 96
HALF = 48
PART = 32
COLS = 384
CHUNKS = 3
SCALE = HEAD_DIM**-0.5 * 1.4426950408889634


def place():
    dp, tm = lax.axis_index("dp"), lax.axis_index("tm")
    return dp // 4, dp % 4, tm // 8, (tm // 2) % 4, tm % 2


def device(y, z, x, core):
    y, z, x = (y + 4) % 4, (z + 16) % 16, (x + 4) % 4
    return (y * 4 + z // 4, (z % 4) * 8 + x * 2 + core)


def remote(src, dst, send, recv, target):
    return pltpu.make_async_remote_copy(
        src_ref=src, dst_ref=dst, send_sem=send, recv_sem=recv, device_id=target, device_id_type=MESH
    )


def kernel(
    x_hbm, w_hbm, start_ref, utt_ref, left_ref, out_hbm,
    xb, wb, qb, kb, vb, ob, masks, acc,
    lx, lw, cs, cr, hs, hr, gs, gr, zs, zr, xs, xr, ys, yr, fs, fr, os_, or_, lo, ready,
):
    y, zh, zl, x, core = place()
    z = zh * 4 + zl
    me = device(y, z, x, core)
    sibling = (me[0], me[1] + 1 - 2 * core)
    y_to = [device(y + 1, z, x, core), device(y + 3, z, x, core)]
    others = [jnp.where(zh == 3, 2 - j, j + jnp.where(j >= zh, 1, 0)) for j in range(3)]
    z_to = [device(y, o * 4 + zl, x, core) for o in others]
    x_to = [device(y, z, x + d, core) for d in (1, 2, 3)]
    groups = [zh] + others
    chip = me[1] // 2
    nxt, prv = (chip + 1) % 16, (chip + 15) % 16

    def rows_of(yy, e, start, count):
        first = ((yy + 4) % 4 * 4 + groups[e]) * DEPTH + start
        return pl.ds(pl.multiple_of(first, 16), count)

    barrier = pltpu.get_barrier_semaphore()

    def greet(target):
        pl.semaphore_signal(barrier, inc=1, device_id=target, device_id_type=MESH)

    own_rows = rows_of(y, 0, 0, DEPTH)

    def own_weights(k, j):
        col = pl.multiple_of(j * 768 + core * 384 + k * 128, 128)
        return pltpu.make_async_copy(
            w_hbm.at[:, pl.ds(col, 128)], wb.at[k, own_rows, pl.ds(j * 128, 128)], lw.at[k, j]
        )

    for k in range(CHUNKS):
        for j in range(3):
            own_weights(k, j).start()
    own_x = pl.ds(pl.multiple_of(REACH + core * ROWS, 16), ROWS)
    own_frames = pltpu.make_async_copy(x_hbm.at[0], xb.at[own_x], lx.at[0])
    own_frames.start()

    has_next = (core == 1) & (chip < 15)
    has_prev = chip > 0
    for t in y_to + x_to + [sibling]:
        greet(t)

    for j in range(3):

        @pl.when((x < 3) & (others[j] > zh))
        def _():
            greet(z_to[j])

    @pl.when(has_prev)
    def _():
        greet((me[0], prv * 2 + 1))

    @pl.when(has_next)
    def _():
        greet((me[0], nxt * 2))
        greet((me[0], nxt * 2 + 1))

    peers = 6 + jnp.where(x < 3, zh, 0) + jnp.where(has_prev, 1, 0) + jnp.where(has_next, 2, 0)
    pl.semaphore_wait(barrier, peers)

    for j in range(3):

        @pl.when((x < 3) & (others[j] < zh))
        def _():
            pl.semaphore_signal(ready.at[zh], inc=1, device_id=z_to[j], device_id_type=MESH)

    def z_copy(k, j, e, source):
        part = wb.at[k, rows_of(y, e, PART * jnp.minimum(x, 2), PART)]
        return remote(part, part, zs.at[k, j], zr.at[k, source], z_to[j])

    def x_copy(k, i, d, owner):
        part = wb.at[k, rows_of(y, i + 1, PART * jnp.minimum(owner, 2), PART)]
        return remote(part, part, xs.at[k, i, d], xr.at[k, i, d], x_to[d])

    def y_copy(k, e, d, yy):
        part = wb.at[k, rows_of(yy, e, 0, DEPTH)]
        return remote(part, part, ys.at[k, e, d], yr.at[k, e, d], y_to[d])

    def f_copy(k, e, d, yy):
        part = wb.at[k, rows_of(yy, e, HALF * d, HALF)]
        return remote(part, part, fs.at[k, e, d], fr.at[k, e, d], y_to[d])

    def z_send(j):
        for k in range(CHUNKS):
            z_copy(k, j, 0, zh).start()

    def z_down():
        for j in range(3):

            @pl.when((x < 3) & (others[j] < zh))
            def _():
                z_send(j)

    def z_up(j):
        @pl.when((x < 3) & (others[j] > zh))
        def _():
            pl.semaphore_wait(ready.at[others[j]], 1)
            z_send(j)

    def y_send(k, e):
        for d in range(2):
            y_copy(k, e, d, y).start()

    def z_to_x(k, j):
        @pl.when(x < 3)
        def _():
            z_copy(k, j, j + 1, others[j]).wait_recv()
            for d in range(3):
                x_copy(k, j, d, x).start()

    def x_to_y(k, j):
        for d in range(3):
            owner = (x + 3 - d) % 4

            @pl.when(owner < 3)
            def _():
                x_copy(k, j, d, owner).wait_recv()

        y_send(k, j + 1)

    def y_to_f(k, e):
        for d in range(2):
            yy = y + (3, 1)[d]
            y_copy(k, e, d, yy).wait_recv()
            f_copy(k, e, d, yy).start()

    def f_end(k, e):
        for d in range(2):
            f_copy(k, e, d, y + 2).wait_recv()

    def halo(i):
        return remote(
            x_hbm.at[0, pl.ds(STRETCH * (i + 1), STRETCH)], xb.at[pl.ds(STRETCH * i, STRETCH)],
            hs.at[i], hr.at[0], (me[0], nxt * 2 + i),
        )

    def halo_across(part_of):
        part = xb.at[pl.ds(pl.multiple_of(STRETCH * part_of, 16), STRETCH)]
        return remote(part, part, gs.at[0], gr.at[0], sibling)

    def to_sibling(rows):
        part = xb.at[pl.ds(pl.multiple_of(REACH + rows * ROWS, 16), ROWS)]
        return remote(x_hbm.at[0], part, cs.at[0], cr.at[0], sibling)

    for k in range(CHUNKS):
        for j in range(3):
            own_weights(k, j).wait()
        y_send(k, 0)
    z_down()
    to_sibling(core).start()

    @pl.when(has_next)
    def _():
        halo(0).start()
        halo(1).start()

    @pl.loop(0, 6)
    def _(b):
        block = chip * 6 + b
        owner = utt_ref[0, block]
        reach = left_ref[0, block]
        start = start_ref[0, owner]
        for d in (2, 1, 0):
            j = block - d
            ok = (j >= 0) & (utt_ref[0, jnp.maximum(j, 0)] == owner) & (reach >= d)
            pos = j * STRETCH + lax.broadcasted_iota(jnp.int32, (1, STRETCH), 1)
            first = jnp.where(ok, start, 1 << 30)
            at = STRETCH * (2 - d)
            masks[pl.ds(b, 1), at : at + STRETCH] = jnp.where(pos >= first, 0.0, -jnp.inf).astype(F32)

    @pl.when(jnp.logical_not(has_prev))
    def _():
        xb[0:REACH] = jnp.zeros((REACH, xb.shape[1]), BF16)

    late = pl.multiple_of(jnp.where(zh == 3, 0, 256), 128)
    soon = pl.multiple_of(256 - late, 128)

    def tiles(ref, k, rr, at):
        if k is None:
            return [ref[rr, pl.ds(pl.multiple_of(yy * 384 + at, 128), 128)] for yy in range(4)]
        return [ref[k, pl.ds(pl.multiple_of(yy * 384 + at, 128), 128), :] for yy in range(4)]

    def project_soon(k, lo_, hi):
        @pl.loop(lo_, hi)
        def _(r):
            rr = pl.ds(pl.multiple_of(r * STRETCH, STRETCH), STRETCH)
            xs_ = jnp.concatenate(tiles(xb, None, rr, 128) + tiles(xb, None, rr, soon), axis=1)
            ws_ = jnp.concatenate(tiles(wb, k, rr, 128) + tiles(wb, k, rr, soon), axis=0)
            acc[k, rr, :] = jnp.dot(xs_, ws_, preferred_element_type=F32)

    def project(k, lo_, hi):
        @pl.loop(lo_, hi)
        def _(r):
            rr = pl.ds(pl.multiple_of(r * STRETCH, STRETCH), STRETCH)
            xs_ = jnp.concatenate(tiles(xb, None, rr, late), axis=1)
            ws_ = jnp.concatenate(tiles(wb, k, rr, late), axis=0)
            p = (acc[k, rr, :] + jnp.dot(xs_, ws_, preferred_element_type=F32)).astype(BF16)
            to = slice(k * 128, (k + 1) * 128)
            qb[rr, to] = p[:, 0:128]
            kb[rr, to] = p[:, 128:256]
            vb[rr, to] = p[:, 256:384]

    lane = lax.broadcasted_iota(jnp.int32, (1, 128), 1)

    def window(h):
        t0, t1 = (h * HEAD_DIM) // 128, (h * HEAD_DIM + HEAD_DIM - 1) // 128
        low, width = h * HEAD_DIM - t0 * 128, (t1 - t0 + 1) * 128
        lanes = lax.broadcasted_iota(jnp.int32, (1, width), 1)
        return slice(t0 * 128, t0 * 128 + width), low, (lanes >= low) & (lanes < low + HEAD_DIM)

    def scores_of(h, b):
        cols, _, mine = window(h)
        rq = pl.ds(pl.multiple_of((b + 2) * STRETCH, STRETCH), STRETCH)
        rk = pl.ds(pl.multiple_of(b * STRETCH, STRETCH), 3 * STRETCH)
        q = jnp.where(mine, qb[rq, cols], jnp.zeros((), BF16))
        return lax.dot_general(q, kb[rk, cols], (((1,), (1,)), ((), ())), preferred_element_type=F32)

    def weights_of(s, bias):
        s = s + bias
        return jnp.exp2((s - jnp.max(s, axis=1, keepdims=True)) * SCALE).astype(BF16)

    def mixed_of(h, b, e, live):
        cols, low, mine = window(h)
        rk = pl.ds(pl.multiple_of(b * STRETCH, STRETCH), 3 * STRETCH)
        v = jnp.where(mine, vb[rk, cols], jnp.ones((), BF16))
        o = jnp.dot(e, v, preferred_element_type=F32)
        one = 0 if low > 0 else HEAD_DIM
        return jnp.where(live, o / o[:, one : one + 1], 0.0).astype(BF16)

    def block_of(b):
        block = chip * 6 + b
        start = start_ref[0, utt_ref[0, block]]
        live = block * STRETCH + lax.broadcasted_iota(jnp.int32, (STRETCH, 1), 0) >= start
        rr = pl.ds(pl.multiple_of(b * STRETCH, STRETCH), STRETCH)
        return live, rr, masks[pl.ds(b, 1), :]

    def out_parts(b, to):
        src = pl.ds(pl.multiple_of(b * STRETCH, STRETCH), STRETCH)
        ro = pl.ds(pl.multiple_of(to * STRETCH, STRETCH), STRETCH)
        return src, out_hbm.at[0, ro, pl.ds(pl.multiple_of(core * COLS, 128), COLS)]

    def attend(lo_, hi):
        @pl.loop(lo_, hi)
        def _(b):
            live, rr, bias = block_of(b)
            heads = range(4)
            scores = [scores_of(h, b) for h in heads]
            shares = [weights_of(s, bias) for s in scores]
            o = [mixed_of(h, b, shares[h], live) for h in heads]
            ob[rr, 0:128] = jnp.where(lane < 96, o[0], o[1][:, :128])
            ob[rr, 128:256] = jnp.where(lane < 64, o[1][:, 128:], o[2][:, :128])
            ob[rr, 256:384] = jnp.where(lane < 32, o[2][:, 128:], o[3])
            i = b % 3
            src, dst = out_parts(b, i)
            here = (b // 3) == core

            @pl.when(here)
            def _():
                pltpu.make_async_copy(ob.at[src], dst, lo.at[i]).start()

            @pl.when(jnp.logical_not(here))
            def _():
                remote(ob.at[src], dst, os_.at[i], or_.at[i], sibling).start()

    z_up(0)
    for k in range(CHUNKS):
        y_to_f(k, 0)
    z_up(1)
    z_up(2)
    for k in range(CHUNKS):
        z_to_x(k, 0)
        z_to_x(k, 1)
    for k in range(CHUNKS):
        x_to_y(k, 0)
        x_to_y(k, 1)
    for k in range(CHUNKS):
        z_to_x(k, 2)
    for k in range(CHUNKS):
        y_to_f(k, 1)
        y_to_f(k, 2)
    for k in range(CHUNKS):
        x_to_y(k, 2)
    own_frames.wait()
    to_sibling(1 - core).wait_recv()
    for k in range(CHUNKS):
        for e in range(3):
            f_end(k, e)
        project_soon(k, 2, 5)
        y_to_f(k, 3)
        project_soon(k, 5, 8)

    @pl.when(has_prev)
    def _():
        part = xb.at[pl.ds(pl.multiple_of(STRETCH * core, 16), STRETCH)]
        remote(part, part, gs.at[0], hr.at[0], sibling).wait_recv()
        halo_across(core).start()

    for k in range(CHUNKS):
        f_end(k, 3)
        project(k, 2, 8)

    @pl.when(has_prev)
    def _():
        halo_across(1 - core).wait_recv()

    for k in range(CHUNKS):
        project_soon(k, 0, 2)
        project(k, 0, 2)
    attend(0, 6)

    for i in range(3):
        src, dst = out_parts(i, i)
        pltpu.make_async_copy(ob.at[src], dst, lo.at[i]).wait()
        other = out_hbm.at[0, pl.ds(i * STRETCH, STRETCH), pl.ds(pl.multiple_of((1 - core) * COLS, 128), COLS)]
        c = remote(ob.at[src], other, os_.at[i], or_.at[i], sibling)
        c.wait_send()
        c.wait_recv()
    for k in range(CHUNKS):
        for e in range(4):
            for d in range(2):
                y_copy(k, e, d, y).wait_send()
                f_copy(k, e, d, y).wait_send()

        @pl.when(x < 3)
        def _():
            for i in range(3):
                z_copy(k, i, 0, zh).wait_send()
                for d in range(3):
                    x_copy(k, i, d, x).wait_send()

    to_sibling(core).wait_send()

    @pl.when(has_next)
    def _():
        halo(0).wait_send()
        halo(1).wait_send()

    @pl.when(has_prev)
    def _():
        halo_across(core).wait_send()


def local(frames, w_qkv, utt_start, stretch_utt, left_stretches):
    any_ = pl.BlockSpec(memory_space=pl.ANY)
    smem = pl.BlockSpec(memory_space=pltpu.SMEM)
    dma = pltpu.SemaphoreType.DMA
    return pl.pallas_call(
        kernel,
        out_shape=jax.ShapeDtypeStruct((1, ROWS, 768), BF16),
        in_specs=[any_, any_, smem, smem, smem],
        out_specs=any_,
        scratch_shapes=[
            pltpu.VMEM((REACH + CHIP, 1536), BF16),
            pltpu.VMEM((CHUNKS, 1536, COLS), BF16),
            pltpu.VMEM((REACH + CHIP, COLS), BF16),
            pltpu.VMEM((REACH + CHIP, COLS), BF16),
            pltpu.VMEM((REACH + CHIP, COLS), BF16),
            pltpu.VMEM((CHIP, COLS), BF16),
            pltpu.VMEM((8, 3 * STRETCH), F32),
            pltpu.VMEM((CHUNKS, REACH + CHIP, COLS), F32),
            dma((1,)), dma((CHUNKS, 3)),
            dma((1,)), dma((1,)), dma((2,)), dma((1,)), dma((1,)), dma((1,)),
            dma((CHUNKS, 3)), dma((CHUNKS, 4)), dma((CHUNKS, 3, 3)), dma((CHUNKS, 3, 3)),
            dma((CHUNKS, 4, 2)), dma((CHUNKS, 4, 2)), dma((CHUNKS, 4, 2)), dma((CHUNKS, 4, 2)),
            dma((3,)), dma((3,)), dma((3,)),
            pltpu.SemaphoreType.REGULAR((4,)),
        ],
        compiler_params=pltpu.CompilerParams(
            collective_id=0, has_side_effects=True, vmem_limit_bytes=60 << 20
        ),
        name="block_attention",
    )(frames, w_qkv, utt_start, stretch_utt, left_stretches)


def solution(mesh):
    return jax.shard_map(
        local,
        mesh=mesh,
        in_specs=(P("dp", "tm", None), P("dp", None), P("dp", None), P("dp", None), P("dp", None)),
        out_specs=P("dp", "tm", None),
        check_vma=False,
    )
```

time: 321 us -> 78.1 us (0.24)
  the two profiles are of different devices: /device:TPU:1 before, /device:TPU:385 now
where the time goes in v2:
time: 78.1 us; the launch traced here: 77.9 us
  Pallas kernels  75.6 us (97%)
  local copies, waits for them, and re-layouts  2.36 us (3%)
    pallas_call x1, Pallas kernels, local(): pl.pallas_call(kernel, out_shape=jax.ShapeDtypeStruct((1, ROWS, 768), BF1...  75.6 us
    unnamed x1, local copies, waits for them, and re-layouts  2.36 us

profile of v2, /device:TPU:385, one launch (start us, length us, event | category | flops | bytes accessed | tf_op | source)
XLA Modules:
  0.0 77.9 jit_solution(870750230027323416)
XLA Ops:
  0.0 75.6 %block_attention.1 = bf16[1,768,768]{2,1,0:T(8,128)(2,1)} custom-call(bf16[1,768,1536]{2,1,0:T(8,128)(2,1)} %x_hbm.1, bf16[96,2304]{1,0:T(8,128)(2,1)} %w_hbm.1, s32[1,24]{1,0:T(1,128)} %start_ref.1, s32[1,96]{1,0:T(1,128)} %utt_ref.1, s32[1,96]{1,0:T(1,128)} %left_ref.1), custom_call_target="tpu_custom_call" | custom-call | tf_op jit(solution)/shard_map/block_attention/pallas_call | solution.py:391
  75.6 2.4 %copy.7 = bf16[1,768,768]{2,1,0:T(8,128)(2,1)} copy(bf16[1,768,768]{2,1,0:T(8,128)(2,1)} %block_attention.1) | data formatting | bytes 2359296

commit v3 on v2

--- a/solution.py
+++ b/solution.py
@@ -40,7 +40,7 @@
 
 def kernel(
     x_hbm, w_hbm, start_ref, utt_ref, left_ref, out_hbm,
-    xb, wb, qb, kb, vb, ob, masks, acc,
+    xb, wb, qb, kb, vb, ob, masks,
     lx, lw, cs, cr, hs, hr, gs, gr, zs, zr, xs, xr, ys, yr, fs, fr, os_, or_, lo, ready,
 ):
     y, zh, zl, x, core = place()
@@ -124,22 +124,26 @@
         part = wb.at[k, rows_of(yy, e, HALF * d, HALF)]
         return remote(part, part, fs.at[k, e, d], fr.at[k, e, d], y_to[d])
 
-    def z_send(j):
+    def z_down():
         for k in range(CHUNKS):
-            z_copy(k, j, 0, zh).start()
-
-    def z_down():
-        for j in range(3):
-
-            @pl.when((x < 3) & (others[j] < zh))
-            def _():
-                z_send(j)
+            for j in range(3):
+
+                @pl.when((x < 3) & (others[j] < zh))
+                def _():
+                    z_copy(k, j, 0, zh).start()
 
     def z_up(j):
         @pl.when((x < 3) & (others[j] > zh))
         def _():
             pl.semaphore_wait(ready.at[others[j]], 1)
-            z_send(j)
+            z_copy(0, j, 0, zh).start()
+
+    def z_more(k):
+        for j in range(3):
+
+            @pl.when((x < 3) & (others[j] > zh))
+            def _():
+                z_copy(k, j, 0, zh).start()
 
     def y_send(k, e):
         for d in range(2):
@@ -216,33 +220,23 @@
     def _():
         xb[0:REACH] = jnp.zeros((REACH, xb.shape[1]), BF16)
 
-    late = pl.multiple_of(jnp.where(zh == 3, 0, 256), 128)
-    soon = pl.multiple_of(256 - late, 128)
-
-    def tiles(ref, k, rr, at):
-        if k is None:
-            return [ref[rr, pl.ds(pl.multiple_of(yy * 384 + at, 128), 128)] for yy in range(4)]
-        return [ref[k, pl.ds(pl.multiple_of(yy * 384 + at, 128), 128), :] for yy in range(4)]
-
-    def project_soon(k, lo_, hi):
-        @pl.loop(lo_, hi)
+    def project(chunks):
+        @pl.loop(0, CHIP // 512)
         def _(r):
-            rr = pl.ds(pl.multiple_of(r * STRETCH, STRETCH), STRETCH)
-            xs_ = jnp.concatenate(tiles(xb, None, rr, 128) + tiles(xb, None, rr, soon), axis=1)
-            ws_ = jnp.concatenate(tiles(wb, k, rr, 128) + tiles(wb, k, rr, soon), axis=0)
-            acc[k, rr, :] = jnp.dot(xs_, ws_, preferred_element_type=F32)
-
-    def project(k, lo_, hi):
-        @pl.loop(lo_, hi)
-        def _(r):
-            rr = pl.ds(pl.multiple_of(r * STRETCH, STRETCH), STRETCH)
-            xs_ = jnp.concatenate(tiles(xb, None, rr, late), axis=1)
-            ws_ = jnp.concatenate(tiles(wb, k, rr, late), axis=0)
-            p = (acc[k, rr, :] + jnp.dot(xs_, ws_, preferred_element_type=F32)).astype(BF16)
-            to = slice(k * 128, (k + 1) * 128)
-            qb[rr, to] = p[:, 0:128]
-            kb[rr, to] = p[:, 128:256]
-            vb[rr, to] = p[:, 256:384]
+            rr = pl.ds(pl.multiple_of(REACH + r * 512, 512), 512)
+            weights = jnp.concatenate([wb[k] for k in chunks], axis=1)
+            p = jnp.dot(xb[rr, :], weights, preferred_element_type=F32).astype(BF16)
+            for n, k in enumerate(chunks):
+                to = slice(k * 128, (k + 1) * 128)
+                for j, ref in enumerate((qb, kb, vb)):
+                    ref[rr, to] = p[:, n * 384 + j * 128 : n * 384 + j * 128 + 128]
+
+    def project_halo():
+        weights = jnp.concatenate([wb[k, :, 128:384] for k in range(CHUNKS)], axis=1)
+        p = jnp.dot(xb[0:REACH, :], weights, preferred_element_type=F32).astype(BF16)
+        for k in range(CHUNKS):
+            kb[0:REACH, k * 128 : (k + 1) * 128] = p[:, k * 256 : k * 256 + 128]
+            vb[0:REACH, k * 128 : (k + 1) * 128] = p[:, k * 256 + 128 : k * 256 + 256]
 
     lane = lax.broadcasted_iota(jnp.int32, (1, 128), 1)
 
@@ -283,55 +277,67 @@
         ro = pl.ds(pl.multiple_of(to * STRETCH, STRETCH), STRETCH)
         return src, out_hbm.at[0, ro, pl.ds(pl.multiple_of(core * COLS, 128), COLS)]
 
-    def attend(lo_, hi):
-        @pl.loop(lo_, hi)
-        def _(b):
-            live, rr, bias = block_of(b)
+    def attend():
+        @pl.loop(0, 6)
+        def _(step):
+            blocks = [lax.rem(step * 1 + n + 3 * (1 - core), 6) for n in range(1)]
             heads = range(4)
-            scores = [scores_of(h, b) for h in heads]
-            shares = [weights_of(s, bias) for s in scores]
-            o = [mixed_of(h, b, shares[h], live) for h in heads]
-            ob[rr, 0:128] = jnp.where(lane < 96, o[0], o[1][:, :128])
-            ob[rr, 128:256] = jnp.where(lane < 64, o[1][:, 128:], o[2][:, :128])
-            ob[rr, 256:384] = jnp.where(lane < 32, o[2][:, 128:], o[3])
-            i = b % 3
-            src, dst = out_parts(b, i)
-            here = (b // 3) == core
-
-            @pl.when(here)
-            def _():
-                pltpu.make_async_copy(ob.at[src], dst, lo.at[i]).start()
-
-            @pl.when(jnp.logical_not(here))
-            def _():
-                remote(ob.at[src], dst, os_.at[i], or_.at[i], sibling).start()
+            each = [block_of(b) for b in blocks]
+            scores = [[scores_of(h, b) for h in heads] for b in blocks]
+            shares = [[weights_of(s, each[n][2]) for s in scores[n]] for n in range(1)]
+            for n, b in enumerate(blocks):
+                live, rr, _ = each[n]
+                o = [mixed_of(h, b, shares[n][h], live) for h in heads]
+                ob[rr, 0:128] = jnp.where(lane < 96, o[0], o[1][:, :128])
+                ob[rr, 128:256] = jnp.where(lane < 64, o[1][:, 128:], o[2][:, :128])
+                ob[rr, 256:384] = jnp.where(lane < 32, o[2][:, 128:], o[3])
+                i = lax.rem(b, 3)
+                src, dst = out_parts(b, i)
+                here = (b // 3) == core
+
+                @pl.when(here)
+                def _(src=src, dst=dst, i=i):
+                    pltpu.make_async_copy(ob.at[src], dst, lo.at[i]).start()
+
+                @pl.when(jnp.logical_not(here))
+                def _(src=src, dst=dst, i=i):
+                    remote(ob.at[src], dst, os_.at[i], or_.at[i], sibling).start()
 
     z_up(0)
     for k in range(CHUNKS):
         y_to_f(k, 0)
     z_up(1)
     z_up(2)
-    for k in range(CHUNKS):
-        z_to_x(k, 0)
-        z_to_x(k, 1)
-    for k in range(CHUNKS):
-        x_to_y(k, 0)
-        x_to_y(k, 1)
-    for k in range(CHUNKS):
-        z_to_x(k, 2)
-    for k in range(CHUNKS):
-        y_to_f(k, 1)
-        y_to_f(k, 2)
-    for k in range(CHUNKS):
-        x_to_y(k, 2)
+    z_to_x(0, 0)
+    z_to_x(0, 1)
+    z_more(1)
+    x_to_y(0, 0)
+    x_to_y(0, 1)
+    z_to_x(0, 2)
+    z_to_x(1, 0)
+    z_to_x(1, 1)
+    z_more(2)
+    x_to_y(0, 2)
+    x_to_y(1, 0)
+    x_to_y(1, 1)
+    y_to_f(0, 1)
+    y_to_f(0, 2)
+    z_to_x(1, 2)
+    z_to_x(2, 0)
+    z_to_x(2, 1)
+    x_to_y(1, 2)
+    x_to_y(2, 0)
+    x_to_y(2, 1)
+    y_to_f(0, 3)
+    y_to_f(1, 1)
+    y_to_f(1, 2)
+    z_to_x(2, 2)
     own_frames.wait()
     to_sibling(1 - core).wait_recv()
-    for k in range(CHUNKS):
-        for e in range(3):
-            f_end(k, e)
-        project_soon(k, 2, 5)
-        y_to_f(k, 3)
-        project_soon(k, 5, 8)
+    y_to_f(1, 3)
+    x_to_y(2, 2)
+    y_to_f(2, 1)
+    y_to_f(2, 2)
 
     @pl.when(has_prev)
     def _():
@@ -339,18 +345,22 @@
         remote(part, part, gs.at[0], hr.at[0], sibling).wait_recv()
         halo_across(core).start()
 
-    for k in range(CHUNKS):
-        f_end(k, 3)
-        project(k, 2, 8)
+    y_to_f(2, 3)
+
+    for k in range(2):
+        for e in range(4):
+            f_end(k, e)
+    project((0, 1))
 
     @pl.when(has_prev)
     def _():
         halo_across(1 - core).wait_recv()
 
-    for k in range(CHUNKS):
-        project_soon(k, 0, 2)
-        project(k, 0, 2)
-    attend(0, 6)
+    for e in range(4):
+        f_end(2, e)
+    project((2,))
+    project_halo()
+    attend()
 
     for i in range(3):
         src, dst = out_parts(i, i)
@@ -401,7 +411,6 @@
             pltpu.VMEM((REACH + CHIP, COLS), BF16),
             pltpu.VMEM((CHIP, COLS), BF16),
             pltpu.VMEM((8, 3 * STRETCH), F32),
-            pltpu.VMEM((CHUNKS, REACH + CHIP, COLS), F32),
             dma((1,)), dma((CHUNKS, 3)),
             dma((1,)), dma((1,)), dma((2,)), dma((1,)), dma((1,)), dma((1,)),
             dma((CHUNKS, 3)), dma((CHUNKS, 4)), dma((CHUNKS, 3, 3)), dma((CHUNKS, 3, 3)),

time: 78.1 us -> 72.9 us (0.933)
  the two profiles are of different devices: /device:TPU:385 before, /device:TPU:32 now
where the time goes in v3:
time: 72.9 us; the launch traced here: 72.8 us
  Pallas kernels  70.4 us (97%)
  local copies, waits for them, and re-layouts  2.36 us (3%)
    pallas_call x1, Pallas kernels, local(): pl.pallas_call(kernel, out_shape=jax.ShapeDtypeStruct((1, ROWS, 768), BF1...  70.4 us
    unnamed x1, local copies, waits for them, and re-layouts  2.36 us

profile of v3, /device:TPU:32, one launch (start us, length us, event | category | flops | bytes accessed | tf_op | source)
XLA Modules:
  0.0 72.8 jit_solution(4297351074239787743)
XLA Ops:
  0.0 70.4 %block_attention.1 = bf16[1,768,768]{2,1,0:T(8,128)(2,1)} custom-call(bf16[1,768,1536]{2,1,0:T(8,128)(2,1)} %x_hbm.1, bf16[96,2304]{1,0:T(8,128)(2,1)} %w_hbm.1, s32[1,24]{1,0:T(1,128)} %start_ref.1, s32[1,96]{1,0:T(1,128)} %utt_ref.1, s32[1,96]{1,0:T(1,128)} %left_ref.1), custom_call_target="tpu_custom_call" | custom-call | tf_op jit(solution)/shard_map/block_attention/pallas_call | solution.py:401
  70.4 2.4 %copy.7 = bf16[1,768,768]{2,1,0:T(8,128)(2,1)} copy(bf16[1,768,768]{2,1,0:T(8,128)(2,1)} %block_attention.1) | data formatting | bytes 2359296

commit v4 on v3

--- a/solution.py
+++ b/solution.py
@@ -126,7 +126,7 @@
 
     def z_down():
         for k in range(CHUNKS):
-            for j in range(3):
+            for j in (2, 1, 0):
 
                 @pl.when((x < 3) & (others[j] < zh))
                 def _():

time: 72.9 us -> 72.7 us (level)
  no operation moved by 1% of the time
where the time goes in v4:
time: 72.7 us; the launch traced here: 72.5 us
  Pallas kernels  70.1 us (96%)
  local copies, waits for them, and re-layouts  2.36 us (3%)
    pallas_call x1, Pallas kernels, local(): pl.pallas_call(kernel, out_shape=jax.ShapeDtypeStruct((1, ROWS, 768), BF1...  70.1 us
    unnamed x1, local copies, waits for them, and re-layouts  2.36 us

profile of v4, /device:TPU:32, one launch (start us, length us, event | category | flops | bytes accessed | tf_op | source)
XLA Modules:
  0.0 72.5 jit_solution(2212400032240455576)
XLA Ops:
  0.0 70.1 %block_attention.1 = bf16[1,768,768]{2,1,0:T(8,128)(2,1)} custom-call(bf16[1,768,1536]{2,1,0:T(8,128)(2,1)} %x_hbm.1, bf16[96,2304]{1,0:T(8,128)(2,1)} %w_hbm.1, s32[1,24]{1,0:T(1,128)} %start_ref.1, s32[1,96]{1,0:T(1,128)} %utt_ref.1, s32[1,96]{1,0:T(1,128)} %left_ref.1), custom_call_target="tpu_custom_call" | custom-call | tf_op jit(solution)/shard_map/block_attention/pallas_call | solution.py:401
  70.1 2.4 %copy.7 = bf16[1,768,768]{2,1,0:T(8,128)(2,1)} copy(bf16[1,768,768]{2,1,0:T(8,128)(2,1)} %block_attention.1) | data formatting | bytes 2359296
